TPU v7x, 128 devices: a whole 4x4x4 slice. The times are simulated.
128 devices in a mesh: arc: 8 (over y, x_hi), trow: 4 (over z), tcol: 4 (over x_lo, core).
Axes of the slice: x: 4 (x_hi: 2, x_lo: 2; x = x_hi * 2 + x_lo), y: 4, z: 4, core: 2. Of those that a mesh axis runs over, the one named last changes fastest.
Arguments:
- design: bfloat16 [5120, 8192], P('arc', 'tcol'), may hold values from -0.125 to 0.125
- local_design: bfloat16 [5120, 128], P('arc'), may hold values from -0.3125 to 0.3125
- lengths: int32 [16], P('arc'), may hold values from 1 to 320, 3840 in all
- regularizer: float32 [8192], P(('arc', 'trow')), may hold values from 0.2 to 2
Outputs:
- normal: float32 [8192, 8192], P(('arc', 'trow'), 'tcol')
- panel_factor: float32 [2, 8192, 512], P(None, 'tcol')
Inputs may be any that keep to these rules, and one draw needn't show every extreme that they name: `lengths`: each arc has at least one live row; some arc is full.
All inputs are finite; a program needn't handle non-finite values. No bound on the sum of `lengths` on one device may be relied on, other than what follows from the above.
Results may differ from a plain program's by a relative error of at most 0.003.
Values may be sent and summed in bfloat16 or wider, within the bound.
A program may use at most 128 MiB of HBM per device.

v0:
```python
import jax
import jax.numpy as jnp
from jax import lax
from jax.sharding import PartitionSpec as P

PANEL = 512
PANELS = 2
ridge = 0.1


def broadcast(block, axis, holder):
    block = jnp.where(lax.axis_index(axis) == holder, block, jnp.zeros_like(block))
    return lax.psum(block, axis)


def project_arcs(design, local_design, lengths):
    arc_count = lengths.shape[0]
    row_count = design.shape[0]
    capacity = row_count // arc_count
    arc_blocks = design.reshape(arc_count, capacity, design.shape[1])
    local_half = local_design.reshape(arc_count, capacity, local_design.shape[1])
    live_rows = jnp.arange(capacity, dtype=jnp.int32)[None, :] < lengths[:, None]
    arc_blocks = jnp.where(live_rows[:, :, None], arc_blocks, jnp.zeros((), design.dtype))
    local_half = jnp.where(live_rows[:, :, None], local_half, jnp.zeros((), local_design.dtype))
    local_normal = jnp.einsum(
        "acl,acm->alm", local_half, local_half, preferred_element_type=jnp.float32
    )
    local_normal = local_normal + ridge * jnp.eye(local_half.shape[2], dtype=jnp.float32)[None]
    local_factor = jnp.linalg.cholesky(local_normal)
    local_cols = local_half.astype(jnp.float32)
    basis_rows = lax.linalg.triangular_solve(
        local_factor, jnp.transpose(local_cols, (0, 2, 1)), left_side=True, lower=True
    )
    basis_rows = basis_rows.astype(jnp.bfloat16)
    loadings = jnp.einsum(
        "alc,acw->alw", basis_rows, arc_blocks, preferred_element_type=jnp.float32
    ).astype(jnp.bfloat16)
    cleaned = arc_blocks.astype(jnp.float32) - jnp.einsum(
        "alc,alw->acw", basis_rows, loadings, preferred_element_type=jnp.float32
    )
    return cleaned.astype(jnp.bfloat16).reshape(row_count, design.shape[1])


def contract_rows(left_rows, right_rows):
    return lax.dot_general(
        left_rows, right_rows, (((0,), (0,)), ((), ())), preferred_element_type=jnp.float32
    )


def per_device(design, local_design, lengths, regularizer):
    row_count, col_width = design.shape
    tile_rows = regularizer.shape[0]
    arc_total = lax.axis_size("arc")
    trow_total = lax.axis_size("trow")
    trow_index = lax.axis_index("trow")
    row_start = (lax.axis_index("arc") * trow_total + trow_index) * tile_rows
    col_start = lax.axis_index("tcol") * col_width
    projected = project_arcs(design, local_design, lengths)
    gathered = lax.all_gather(projected, "tcol", axis=1, tiled=True)
    regrouped = gathered.reshape(row_count, arc_total, trow_total, tile_rows)
    selected = lax.dynamic_slice_in_dim(regrouped, trow_index, 1, 2).reshape(
        row_count, arc_total * tile_rows
    )
    normal_block = lax.psum_scatter(
        contract_rows(selected, projected), "arc", scatter_dimension=0, tiled=True
    )
    rows_global = row_start + jnp.arange(tile_rows, dtype=jnp.int32)
    cols_global = col_start + jnp.arange(col_width, dtype=jnp.int32)
    on_diagonal = rows_global[:, None] == cols_global[None, :]
    normal_block = normal_block + jnp.where(
        on_diagonal, regularizer[:, None], jnp.zeros((), jnp.float32)
    )
    panel_factors = []
    for panel_index in range(PANELS):
        lead_col = panel_index * PANEL
        padded_rows = jnp.pad(normal_block, ((PANEL, PANEL), (0, 0)))
        slice_start = jnp.clip(lead_col - row_start + PANEL, 0, tile_rows + PANEL)
        slice_rows = lax.dynamic_slice_in_dim(padded_rows, slice_start, PANEL, 0)
        panel_global = lead_col + jnp.arange(PANEL, dtype=jnp.int32)
        in_tile = (panel_global >= row_start) & (panel_global < row_start + tile_rows)
        own_share = jnp.where(in_tile[:, None], slice_rows, jnp.zeros((), jnp.float32))
        panel_strip = lax.psum(own_share, ("arc", "trow"))
        pivot_block, row_strip = (
            broadcast(panel_strip[:, lead_col : lead_col + PANEL], "tcol", 0),
            broadcast(normal_block[:, lead_col : lead_col + PANEL], "tcol", 0),
        )
        lower_factor = jnp.linalg.cholesky(pivot_block)
        col_factor = lax.linalg.triangular_solve(
            lower_factor, panel_strip, left_side=True, lower=True
        ).T
        row_factor = lax.linalg.triangular_solve(
            lower_factor, row_strip.T, left_side=True, lower=True
        ).T
        col_factor = jnp.where(
            cols_global[:, None] >= lead_col, col_factor, jnp.zeros((), jnp.float32)
        )
        row_factor = jnp.where(
            rows_global[:, None] >= lead_col, row_factor, jnp.zeros((), jnp.float32)
        )
        normal_block = normal_block - jnp.dot(
            row_factor, col_factor.T, precision=lax.Precision.HIGHEST
        )
        panel_factors.append(col_factor)
    return (normal_block, jnp.stack(panel_factors))


def solution(mesh):
    return jax.shard_map(
        per_device,
        mesh=mesh,
        in_specs=(P("arc", "tcol"), P("arc", None), P("arc"), P(("arc", "trow"))),
        out_specs=(P(("arc", "trow"), "tcol"), P(None, "tcol", None)),
        check_vma=False,
    )
```

profile of v0, /device:TPU:1, one launch (start us, length us, event | category | flops | bytes accessed | tf_op | source)
XLA Modules:
  0.0 1569.1 jit_solution(3386765637183662593)
XLA Ops:
  9.6 23.5 %custom-call.33 = f32[2,128,128]{2,1,0:T(8,128)S(1)} custom-call(f32[2,128,128]{2,1,0:T(8,128)S(1)} %fusion.97), custom_call_target="Cholesky" | custom-call | tf_op jit(solution)/shard_map/jit(cholesky)/cholesky | solution.py:29
  33.4 19.7 %custom-call.34 = f32[2,1,128,128]{2,3,1,0:T(8,128)S(1)} custom-call(f32[2,1,128,128]{3,2,1,0:T(8,128)S(1)} %select_bitcast_fusion), custom_call_target="InvertDiagBlocksLowerTriangular" | custom-call | tf_op jit(solution)/shard_map/triangular_solve | solution.py:31
  61.2 102.4 %all-gather.2.cloned.1.call-done = bf16[640,8192]{0,1:T(8,128)(2,1)} async-done(((bf16[640,2048]{0,1:T(8,128)(2,1)}), bf16[640,8192]{0,1:T(8,128)(2,1)}) %all-gather.2.cloned.1.call-update) | async-done | bytes 10485776 | tf_op jit(solution)/shard_map/all_gather | solution.py:59
  165.6 10.2 fusion.158
  175.9 190.4 %reduce-scatter.2.cloned.1.call-done = f32[256,2048]{0,1:T(8,128)} async-done(((f32[2048,2048]{0,1:T(8,128)}), f32[256,2048]{0,1:T(8,128)}) %reduce-scatter.2.cloned.1.call-update) | async-done | bytes 2097168 | tf_op jit(solution)/shard_map/reduce_scatter | solution.py:64
  372.1 345.6 %all-reduce.10.cloned.1.call-done = f32[512,2048]{0,1:T(8,128)} async-done(((f32[512,2048]{0,1:T(8,128)}), f32[512,2048]{0,1:T(8,128)}) %all-reduce.10.cloned.1.call-update) | async-done | bytes 4194320 | tf_op jit(solution)/shard_map/psum | solution.py:82
  720.2 71.5 %all-reduce.16.cloned.1.call-done = (f32[512,512]{0,1:T(8,128)}, f32[512,256]{1,0:T(8,128)}) async-done(((f32[512,512]{0,1:T(8,128)}, f32[512,256]{1,0:T(8,128)}), (f32[512,512]{0,1:T(8,128)}, f32[512,256]{1,0:T(8,128)})) %all-reduce.16.cloned.1.call-update) | async-done | bytes 1572880 | tf_op jit(solution)/shard_map/psum | solution.py:13
  794.7 11.7 cholesky.327
  806.6 9.8 custom-call.40
  817.1 11.7 cholesky.346
  828.8 10.2 custom-call.41
  839.7 11.7 cholesky.367
  851.5 9.8 custom-call.42
  861.9 11.7 cholesky.384
  886.6 39.3 %custom-call.43 = f32[4,128,128]{1,2,0:T(8,128)S(1)} custom-call(f32[4,128,128]{2,1,0:T(8,128)S(1)} %get-tuple-element.33), custom_call_target="InvertDiagBlocksLowerTriangular" | custom-call | tf_op jit(solution)/shard_map/triangular_solve/custom-call.9 | solution.py:91
  966.0 342.8 %all-reduce.12.cloned.1.call-done = f32[512,2048]{0,1:T(8,128)} async-done(((f32[512,2048]{0,1:T(8,128)}), f32[512,2048]{0,1:T(8,128)}) %all-reduce.12.cloned.1.call-update) | async-done | bytes 4194320 | tf_op jit(solution)/shard_map/psum | solution.py:82
  1314.6 68.2 %all-reduce.14.cloned.1.call-done = (f32[512,512]{0,1:T(8,128)}, f32[512,256]{1,0:T(8,128)}) async-done(((f32[512,512]{0,1:T(8,128)}, f32[512,256]{1,0:T(8,128)}), (f32[512,512]{0,1:T(8,128)}, f32[512,256]{1,0:T(8,128)})) %all-reduce.14.cloned.1.call-update) | async-done | bytes 1572880 | tf_op jit(solution)/shard_map/psum | solution.py:13
  1385.7 11.7 cholesky.399
  1408.1 11.7 cholesky.418
  1419.8 10.2 custom-call.46
  1430.7 11.7 cholesky.439
  1442.5 9.8 custom-call.47
  1452.9 11.7 cholesky.456
  1477.6 39.3 %custom-call.48 = f32[4,128,128]{1,2,0:T(8,128)S(1)} custom-call(f32[4,128,128]{2,1,0:T(8,128)S(1)} %get-tuple-element.35), custom_call_target="InvertDiagBlocksLowerTriangular" | custom-call | tf_op jit(solution)/shard_map/triangular_solve/custom-call.9 | solution.py:91
  (192 shorter events, 168.0 us)
Async XLA Ops:
  7.2 156.4 %all-gather.2.cloned.1.call-start = ((), (), s32[]{:S(2)}) async-start(), calls=%async_computation.1 | async-start | bytes 13107200 | tf_op jit(solution)/shard_map/all_gather | solution.py:59
  61.0 305.3 %reduce-scatter.2.cloned.1.call-start = ((), (), s32[]{:S(2)}) async-start(), calls=%async_computation.2 | async-start | bytes 18874368 | tf_op jit(solution)/shard_map/reduce_scatter | solution.py:64
  175.8 190.5 %copy-start.18 = (f32[256]{0:T(256)S(1)}, f32[256]{0:T(256)}, u32[]{:S(2)}) copy-start(f32[256]{0:T(256)} %param.12) | copy-start | bytes 3076
  175.8 542.0 %all-reduce.10.cloned.1.call-start = ((), (), s32[]{:S(2)}) async-start(), calls=%async_computation.3 | async-start | bytes 8388608 | tf_op jit(solution)/shard_map/psum | solution.py:82
  368.0 3.3 copy-start
  371.2 420.5 %all-reduce.16.cloned.1.call-start = ((), (), s32[]{:S(2)}) async-start(), calls=%async_computation.6 | async-start | bytes 3145728 | tf_op jit(solution)/shard_map/psum | solution.py:13
  720.1 588.7 %all-reduce.12.cloned.1.call-start = ((), (), s32[]{:S(2)}) async-start(), calls=%async_computation.4 | async-start | bytes 8388608 | tf_op jit(solution)/shard_map/psum | solution.py:82
  886.6 48.4 %copy-start.3 = (f32[512,512]{1,0:T(8,128)}, f32[512,512]{1,0:T(8,128)S(1)}, u32[]{:S(2)}) copy-start(f32[512,512]{1,0:T(8,128)S(1)} %get-tuple-element.206) | copy-start | bytes 3145732
  942.2 8.3 copy-start.16
  942.2 13.2 copy-start.1
  942.2 13.2 copy-start.4
  942.2 13.2 copy-start.6
  942.2 13.2 copy-start.8
  950.5 8.9 copy-start.10
  963.9 347.3 %copy-start.5 = (f32[128,2048]{0,1:T(8,128)S(1)}, f32[128,2048]{0,1:T(8,128)}, u32[]{:S(2)}) copy-start(f32[128,2048]{0,1:T(8,128)} %copy.69) | copy-start | bytes 3145732
  963.9 347.3 %copy-start.7 = (f32[128,2048]{0,1:T(8,128)S(1)}, f32[128,2048]{0,1:T(8,128)}, u32[]{:S(2)}) copy-start(f32[128,2048]{0,1:T(8,128)} %copy.70) | copy-start | bytes 3145732
  963.9 347.3 %copy-start.9 = (f32[128,2048]{0,1:T(8,128)S(1)}, f32[128,2048]{0,1:T(8,128)}, u32[]{:S(2)}) copy-start(f32[128,2048]{0,1:T(8,128)} %copy.71) | copy-start | bytes 3145732
  963.9 418.8 %all-reduce.14.cloned.1.call-start = ((), (), s32[]{:S(2)}) async-start(), calls=%async_computation.5 | async-start | bytes 3145728 | tf_op jit(solution)/shard_map/psum | solution.py:13
  1477.6 48.4 %copy-start.2 = (f32[512,512]{1,0:T(8,128)}, f32[512,512]{1,0:T(8,128)S(1)}, u32[]{:S(2)}) copy-start(f32[512,512]{1,0:T(8,128)S(1)} %get-tuple-element.205) | copy-start | bytes 3145732
  1533.2 8.1 copy-start.17
  1533.2 13.0 copy-start.11
  1533.2 13.0 copy-start.12
  1533.2 13.0 copy-start.13
  1546.2 2.5 copy-start.15
  (1 other events, 1.3 us)
Sparse Core Ops, SparseCore 0:
  61.1 102.4 all-gather.1
  175.9 190.3 reduce-scatter.1
  371.4 346.3 all-reduce.9
  721.0 70.6 all-reduce.15
  964.0 344.7 all-reduce.11
  1312.0 70.6 all-reduce.13
where the time goes:
time: 1580 us; the launch traced here: 1570 us
  waiting for transfers between devices  1120 us (71%)
  other arithmetic  314 us (20%)
  matrix products  78.7 us (5%)
  local copies, waits for them, and re-layouts  34.9 us (2%)
  between operations  20 us (1%)
    psum x2, waiting for transfers between devices, per_device(): panel_strip = lax.psum(own_share, ('arc', 'trow'))  688 us
    reduce_scatter x1, waiting for transfers between devices, per_device(): lax.psum_scatter(contract_rows(selected, projected), 'arc', scatter_dimen...  190 us
    another operation x30, other arithmetic, per_device(): lower_factor = jnp.linalg.cholesky(pivot_block)  159 us
    psum x2, waiting for transfers between devices, broadcast(): return lax.psum(block, axis)  140 us
    all_gather x1, waiting for transfers between devices, per_device(): gathered = lax.all_gather(projected, 'tcol', axis=1, tiled=True)  102 us
    another operation x5, other arithmetic, per_device(): lax.linalg.triangular_solve(lower_factor, row_strip.T, left_side=True, lo...  79.2 us
    another operation x14, matrix products, per_device(): lax.linalg.triangular_solve(lower_factor, panel_strip, left_side=True, lo...  40.7 us
  transfers between devices with their start and end apart: 6, of which 6 were waited for; matrix products, arithmetic and copies ran while one was open for 0% of the time, Pallas kernels for 0%

commit v1 on v0

--- a/solution.py
+++ b/solution.py
@@ -79,7 +79,7 @@
         panel_global = lead_col + jnp.arange(PANEL, dtype=jnp.int32)
         in_tile = (panel_global >= row_start) & (panel_global < row_start + tile_rows)
         own_share = jnp.where(in_tile[:, None], slice_rows, jnp.zeros((), jnp.float32))
-        panel_strip = lax.psum(own_share, ("arc", "trow"))
+        panel_strip = lax.psum(lax.psum(own_share, "arc"), "trow")
         pivot_block, row_strip = (
             broadcast(panel_strip[:, lead_col : lead_col + PANEL], "tcol", 0),
             broadcast(normal_block[:, lead_col : lead_col + PANEL], "tcol", 0),

time: 1580 us -> 1410 us (0.89)
  waiting for transfers between devices: 1120 us -> 948 us
    psum x2 -> x4, waiting for transfers between devices: 688 us -> 559 us  [per_device(): panel_strip = lax.psum(lax.psum(own_share, 'arc'), 'trow')]
    psum x2, waiting for transfers between devices: 140 us -> 96.2 us  [broadcast(): return lax.psum(block, axis)]
  transfers between devices with their start and end apart: 6 -> 8, of which waited for: 6 -> 8; matrix products, arithmetic and copies ran while one was open for 0% -> 0% of each run, Pallas kernels for 0% -> 0%
where the time goes in v1:
time: 1410 us; the launch traced here: 1400 us
  waiting for transfers between devices  948 us (67%)
  other arithmetic  314 us (22%)
  matrix products  78.7 us (6%)
  local copies, waits for them, and re-layouts  35.5 us (3%)
  between operations  20.3 us (1%)
    psum x4, waiting for transfers between devices, per_device(): panel_strip = lax.psum(lax.psum(own_share, 'arc'), 'trow')  559 us
    reduce_scatter x1, waiting for transfers between devices, per_device(): lax.psum_scatter(contract_rows(selected, projected), 'arc', scatter_dimen...  190 us
    another operation x30, other arithmetic, per_device(): lower_factor = jnp.linalg.cholesky(pivot_block)  159 us
    all_gather x1, waiting for transfers between devices, per_device(): gathered = lax.all_gather(projected, 'tcol', axis=1, tiled=True)  102 us
    psum x2, waiting for transfers between devices, broadcast(): return lax.psum(block, axis)  96.2 us
    another operation x5, other arithmetic, per_device(): lax.linalg.triangular_solve(lower_factor, row_strip.T, left_side=True, lo...  79.2 us
    another operation x14, matrix products, per_device(): lax.linalg.triangular_solve(lower_factor, panel_strip, left_side=True, lo...  40.7 us
  transfers between devices with their start and end apart: 8, of which 8 were waited for; matrix products, arithmetic and copies ran while one was open for 0% of the time, Pallas kernels for 0%

profile of v1, /device:TPU:1, one launch (start us, length us, event | category | flops | bytes accessed | tf_op | source)
XLA Modules:
  0.0 1397.5 jit_solution(984631654632649256)
XLA Ops:
  9.6 23.5 %custom-call.33 = f32[2,128,128]{2,1,0:T(8,128)S(1)} custom-call(f32[2,128,128]{2,1,0:T(8,128)S(1)} %fusion.97), custom_call_target="Cholesky" | custom-call | tf_op jit(solution)/shard_map/jit(cholesky)/cholesky | solution.py:29
  33.4 19.7 %custom-call.34 = f32[2,1,128,128]{2,3,1,0:T(8,128)S(1)} custom-call(f32[2,1,128,128]{3,2,1,0:T(8,128)S(1)} %select_bitcast_fusion), custom_call_target="InvertDiagBlocksLowerTriangular" | custom-call | tf_op jit(solution)/shard_map/triangular_solve | solution.py:31
  61.2 102.4 %all-gather.2.cloned.1.call-done = bf16[640,8192]{0,1:T(8,128)(2,1)} async-done(((bf16[640,2048]{0,1:T(8,128)(2,1)}), bf16[640,8192]{0,1:T(8,128)(2,1)}) %all-gather.2.cloned.1.call-update) | async-done | bytes 10485776 | tf_op jit(solution)/shard_map/all_gather | solution.py:59
  165.6 10.2 fusion.158
  175.9 190.4 %reduce-scatter.2.cloned.1.call-done = f32[256,2048]{0,1:T(8,128)} async-done(((f32[2048,2048]{0,1:T(8,128)}), f32[256,2048]{0,1:T(8,128)}) %reduce-scatter.2.cloned.1.call-update) | async-done | bytes 2097168 | tf_op jit(solution)/shard_map/reduce_scatter | solution.py:64
  371.3 187.1 %all-reduce.12.cloned.1.call-done = f32[512,2048]{0,1:T(8,128)} async-done(((f32[512,2048]{0,1:T(8,128)}), f32[512,2048]{0,1:T(8,128)}) %all-reduce.12.cloned.1.call-update) | async-done | bytes 4194320 | tf_op jit(solution)/shard_map/psum | solution.py:82
  559.4 93.8 %all-reduce.14.cloned.1.call-done = f32[512,2048]{0,1:T(8,128)} async-done(((f32[512,2048]{0,1:T(8,128)}), f32[512,2048]{0,1:T(8,128)}) %all-reduce.14.cloned.1.call-update) | async-done | bytes 4194320 | tf_op jit(solution)/shard_map/psum | solution.py:82
  655.8 49.5 %all-reduce.22.cloned.1.call-done = (f32[512,512]{0,1:T(8,128)}, f32[512,256]{1,0:T(8,128)}) async-done(((f32[512,512]{0,1:T(8,128)}, f32[512,256]{1,0:T(8,128)}), (f32[512,512]{0,1:T(8,128)}, f32[512,256]{1,0:T(8,128)})) %all-reduce.22.cloned.1.call-update) | async-done | bytes 1572880 | tf_op jit(solution)/shard_map/psum | solution.py:13
  708.4 11.7 cholesky.327
  730.7 11.7 cholesky.346
  742.5 10.2 custom-call.41
  753.4 11.7 cholesky.367
  765.1 9.8 custom-call.42
  775.6 11.7 cholesky.384
  800.8 39.3 %custom-call.43 = f32[4,128,128]{1,2,0:T(8,128)S(1)} custom-call(f32[4,128,128]{2,1,0:T(8,128)S(1)} %get-tuple-element.33), custom_call_target="InvertDiagBlocksLowerTriangular" | custom-call | tf_op jit(solution)/shard_map/triangular_solve/custom-call.9 | solution.py:91
  878.1 185.3 %all-reduce.16.cloned.1.call-done = f32[512,2048]{0,1:T(8,128)} async-done(((f32[512,2048]{0,1:T(8,128)}), f32[512,2048]{0,1:T(8,128)}) %all-reduce.16.cloned.1.call-update) | async-done | bytes 4194320 | tf_op jit(solution)/shard_map/psum | solution.py:82
  1065.5 92.7 %all-reduce.18.cloned.1.call-done = f32[512,2048]{0,1:T(8,128)} async-done(((f32[512,2048]{0,1:T(8,128)}), f32[512,2048]{0,1:T(8,128)}) %all-reduce.18.cloned.1.call-update) | async-done | bytes 4194320 | tf_op jit(solution)/shard_map/psum | solution.py:82
  1164.0 46.7 %all-reduce.20.cloned.1.call-done = (f32[512,512]{0,1:T(8,128)}, f32[512,256]{1,0:T(8,128)}) async-done(((f32[512,512]{0,1:T(8,128)}, f32[512,256]{1,0:T(8,128)}), (f32[512,512]{0,1:T(8,128)}, f32[512,256]{1,0:T(8,128)})) %all-reduce.20.cloned.1.call-update) | async-done | bytes 1572880 | tf_op jit(solution)/shard_map/psum | solution.py:13
  1213.7 11.7 cholesky.399
  1236.0 11.7 cholesky.418
  1247.8 10.2 custom-call.46
  1258.7 11.7 cholesky.439
  1280.8 11.7 cholesky.456
  1306.1 39.3 %custom-call.48 = f32[4,128,128]{1,2,0:T(8,128)S(1)} custom-call(f32[4,128,128]{2,1,0:T(8,128)S(1)} %get-tuple-element.35), custom_call_target="InvertDiagBlocksLowerTriangular" | custom-call | tf_op jit(solution)/shard_map/triangular_solve/custom-call.9 | solution.py:91
  (198 shorter events, 189.3 us)
Async XLA Ops:
  7.2 156.4 %all-gather.2.cloned.1.call-start = ((), (), s32[]{:S(2)}) async-start(), calls=%async_computation.1 | async-start | bytes 13107200 | tf_op jit(solution)/shard_map/all_gather | solution.py:59
  61.0 305.3 %reduce-scatter.2.cloned.1.call-start = ((), (), s32[]{:S(2)}) async-start(), calls=%async_computation.2 | async-start | bytes 18874368 | tf_op jit(solution)/shard_map/reduce_scatter | solution.py:64
  175.8 190.5 %copy-start.18 = (f32[256]{0:T(256)S(1)}, f32[256]{0:T(256)}, u32[]{:S(2)}) copy-start(f32[256]{0:T(256)} %param.12) | copy-start | bytes 3076
  175.8 382.7 %all-reduce.12.cloned.1.call-start = ((), (), s32[]{:S(2)}) async-start(), calls=%async_computation.3 | async-start | bytes 8388608 | tf_op jit(solution)/shard_map/psum | solution.py:82
  368.0 190.5 %copy-start = (f32[256,2048]{0,1:T(8,128)}, f32[256,2048]{0,1:T(8,128)S(1)}, u32[]{:S(2)}) copy-start(f32[256,2048]{0,1:T(8,128)S(1)} %select_add_fusion) | copy-start | bytes 6291460
  371.2 282.0 %all-reduce.14.cloned.1.call-start = ((), (), s32[]{:S(2)}) async-start(), calls=%async_computation.4 | async-start | bytes 8388608 | tf_op jit(solution)/shard_map/psum | solution.py:82
  558.5 146.9 %all-reduce.22.cloned.1.call-start = ((), (), s32[]{:S(2)}) async-start(), calls=%async_computation.8 | async-start | bytes 3145728 | tf_op jit(solution)/shard_map/psum | solution.py:13
  655.5 407.9 %all-reduce.16.cloned.1.call-start = ((), (), s32[]{:S(2)}) async-start(), calls=%async_computation.5 | async-start | bytes 8388608 | tf_op jit(solution)/shard_map/psum | solution.py:82
  800.8 48.4 %copy-start.3 = (f32[512,512]{1,0:T(8,128)}, f32[512,512]{1,0:T(8,128)S(1)}, u32[]{:S(2)}) copy-start(f32[512,512]{1,0:T(8,128)S(1)} %get-tuple-element.208) | copy-start | bytes 3145732
  856.4 8.3 copy-start.16
  856.4 13.2 copy-start.1
  856.4 13.2 copy-start.4
  856.4 13.2 copy-start.6
  856.4 13.2 copy-start.8
  864.6 8.9 copy-start.10
  878.1 280.1 %all-reduce.18.cloned.1.call-start = ((), (), s32[]{:S(2)}) async-start(), calls=%async_computation.6 | async-start | bytes 8388608 | tf_op jit(solution)/shard_map/psum | solution.py:82
  1063.4 97.1 %copy-start.5 = (f32[128,2048]{0,1:T(8,128)S(1)}, f32[128,2048]{0,1:T(8,128)}, u32[]{:S(2)}) copy-start(f32[128,2048]{0,1:T(8,128)} %copy.69) | copy-start | bytes 3145732
  1063.4 97.1 %copy-start.7 = (f32[128,2048]{0,1:T(8,128)S(1)}, f32[128,2048]{0,1:T(8,128)}, u32[]{:S(2)}) copy-start(f32[128,2048]{0,1:T(8,128)} %copy.70) | copy-start | bytes 3145732
  1063.4 97.1 %copy-start.9 = (f32[128,2048]{0,1:T(8,128)S(1)}, f32[128,2048]{0,1:T(8,128)}, u32[]{:S(2)}) copy-start(f32[128,2048]{0,1:T(8,128)} %copy.71) | copy-start | bytes 3145732
  1063.4 147.2 %all-reduce.20.cloned.1.call-start = ((), (), s32[]{:S(2)}) async-start(), calls=%async_computation.7 | async-start | bytes 3145728 | tf_op jit(solution)/shard_map/psum | solution.py:13
  1306.0 48.4 %copy-start.2 = (f32[512,512]{1,0:T(8,128)}, f32[512,512]{1,0:T(8,128)S(1)}, u32[]{:S(2)}) copy-start(f32[512,512]{1,0:T(8,128)S(1)} %get-tuple-element.207) | copy-start | bytes 3145732
  1361.7 13.0 copy-start.11
  1361.7 13.0 copy-start.12
  1361.7 13.0 copy-start.13
  (3 other events, 11.9 us)
Sparse Core Ops, SparseCore 0:
  61.1 102.4 all-gather.1
  175.9 190.3 reduce-scatter.1
  371.4 187.0 all-reduce.11
  560.8 92.3 all-reduce.13
  656.2 49.0 all-reduce.21
  878.2 185.1 all-reduce.15
  1065.8 92.3 all-reduce.17
  1161.5 49.0 all-reduce.19
